TPU v7x, 128 devices: a whole 4x4x4 slice. The times are simulated.
128 devices in a mesh: surf: 4 (over z_hi, core), shot: 32 (over z_lo, x, y).
Axes of the slice: x: 4, y: 4, z: 4 (z_hi: 2, z_lo: 2; z = z_hi * 2 + z_lo), core: 2. Of those that a mesh axis runs over, the one named last changes fastest.
Arguments:
- traces: bfloat16 [256, 640, 1024], P('shot'), may hold values from -6 to 6
- surface_point: int32 [4, 4, 2], replicated, may hold values from 0 to 639, as said below
- gather_index: int32 [4, 4, 2], replicated, may hold values from 0 to 255, as said below
Outputs:
- prediction: bfloat16 [256, 640, 1024], P('shot', 'surf')
Inputs may be any that keep to these rules, and one draw needn't show every extreme that they name: `surface_point`: all 32 entries are distinct. `gather_index`: the 2 entries of one round and group are distinct and lie on one index of shot: they share their quotient by 8.
All inputs are finite; a program needn't handle non-finite values.
Results may differ from a plain program's by a relative error of at most 0.015.
Values may be sent and summed in bfloat16 or wider, within the bound.
A program may use at most 128 MiB of HBM per device.

v0:
```python
import math

import jax
import jax.numpy as jnp
from jax import lax
from jax.sharding import PartitionSpec as P

F = 256


def spread(array, axis, root):
    mine = lax.axis_index(axis) == root
    return lax.psum(jnp.where(mine, array, jnp.zeros_like(array)), axis)


def dft_table(samples, freq_bins):
    time_index = jnp.arange(samples, dtype=jnp.int32)[:, None]
    freq_index = jnp.arange(freq_bins, dtype=jnp.int32)[None, :]
    phase_int = time_index * freq_index % samples
    angles = phase_int.astype(jnp.float32) * (2.0 * math.pi / samples)
    return jnp.concatenate([jnp.cos(angles), -jnp.sin(angles)], axis=1).astype(jnp.bfloat16)


def spectral_product(near_spec, far_spec, half_bins):
    near_real = near_spec[..., :half_bins]
    near_imag = near_spec[..., half_bins:]
    far_real = far_spec[..., :half_bins]
    far_imag = far_spec[..., half_bins:]
    left_real = jnp.concatenate([near_real, -near_imag], axis=1)
    right_real = jnp.concatenate([far_real, far_imag], axis=0)
    left_imag = jnp.concatenate([near_real, near_imag], axis=1)
    right_imag = jnp.concatenate([far_imag, far_real], axis=0)
    real_part = jnp.einsum(
        "skf,krf->srf", left_real, right_real, preferred_element_type=jnp.float32
    )
    imag_part = jnp.einsum(
        "skf,krf->srf", left_imag, right_imag, preferred_element_type=jnp.float32
    )
    return jnp.concatenate([real_part, imag_part], axis=2)


def transform(gathers, forward, factor):
    return (jnp.dot(gathers, forward, preferred_element_type=jnp.float32) * factor).astype(
        jnp.bfloat16
    )


def share_round(block, source_rank, forward, factor):
    arrived = spread(block, "shot", source_rank)
    return transform(arrived, forward, factor)


def shards(traces, surface_point, gather_index):
    shot_dev, receivers, samples = traces.shape
    forward = dft_table(samples, F)
    factor = samples ** (-0.5)
    group_index = lax.axis_index("surf")
    round_count = surface_point.shape[0]
    points = jnp.take(surface_point, group_index, axis=1).reshape(-1)
    sources = jnp.take(gather_index, group_index, axis=1)
    columns = jnp.take(traces, points, axis=1)
    near_spec = transform(columns, forward, factor)
    far_parts = []
    for round_index in range(round_count):
        wanted = sources[round_index]
        source_rank = wanted[0] // shot_dev
        picked = jnp.take(traces, wanted % shot_dev, axis=0)
        far_parts.append(share_round(picked, source_rank, forward, factor))
    far_spec = jnp.concatenate(far_parts, axis=0)
    partial_value = spectral_product(near_spec, far_spec, F).astype(jnp.bfloat16)
    partial_value = lax.optimization_barrier(partial_value)
    partial_value = partial_value.astype(jnp.float32)
    summed = lax.psum_scatter(
        partial_value.astype(jnp.bfloat16), "surf", scatter_dimension=1, tiled=True
    )
    result = lax.dot_general(
        summed, forward, (((2,), (1,)), ((), ())), preferred_element_type=jnp.float32
    )
    return (result * -factor).astype(jnp.bfloat16)


def solution(mesh):
    placed = (P("shot", None, None), P(), P())
    return jax.shard_map(
        shards, mesh=mesh, in_specs=placed, out_specs=P("shot", "surf", None), check_vma=False
    )
```

profile of v0, /device:TPU:1, one launch (start us, length us, event | category | flops | bytes accessed | tf_op | source)
XLA Modules:
  0.0 534.9 jit_solution(1460260321555235828)
XLA Ops:
  6.5 0.8 dynamic-slice_select_fusion.1
  7.3 0.1 copy.8
  7.4 0.7 fusion.18
  10.0 0.2 slice_reduce_fusion.3
  18.6 6.2 %gather_fusion.2 = bf16[2,640,1024]{2,1,0:T(8,128)(2,1)} fusion(bf16[8,640,1024]{2,1,0:T(8,128)(2,1)} %param.7, s32[1024]{0:T(1024)S(1)} %pad_clamp_fusion.3), kind=kCustom, calls=%fused_computation.1.clone | custom fusion | bytes 5242888 | tf_op jit(solution)/shard_map/jit(_take)/gather | solution.py:67
  24.7 4.7 gather_fusion.1
  29.5 6.2 %gather_fusion.3 = bf16[2,640,1024]{2,1,0:T(8,128)(2,1)} fusion(bf16[8,640,1024]{2,1,0:T(8,128)(2,1)} %param.7, s32[1024]{0:T(1024)S(1)} %pad_clamp_fusion.2), kind=kCustom, calls=%fused_computation.2.clone | custom fusion | bytes 5242888 | tf_op jit(solution)/shard_map/jit(_take)/gather | solution.py:67
  35.7 6.2 %gather_fusion.4 = bf16[2,640,1024]{2,1,0:T(8,128)(2,1)} fusion(bf16[8,640,1024]{2,1,0:T(8,128)(2,1)} %param.7, s32[1024]{0:T(1024)S(1)} %pad_clamp_fusion.1), kind=kCustom, calls=%fused_computation.3.clone | custom fusion | bytes 5242888 | tf_op jit(solution)/shard_map/jit(_take)/gather | solution.py:67
  41.9 3.6 select_select_fusion.2
  45.5 1.9 select_select_fusion.3
  47.3 0.8 copy-done
  48.1 1.8 select_select_fusion.1
  49.9 0.9 copy-done.1
  50.8 1.8 select_select_fusion
  52.7 0.0 all-reduce.3.cloned.1.call-update
  52.7 0.2 reduce-scatter.2.cloned.1.call-start
  52.9 0.4 copy-done.7
  53.4 0.1 dynamic-slice_select_fusion
  53.4 0.1 copy.9
  53.5 0.1 copy.10
  53.6 0.1 reshape.54
  53.7 0.1 reshape.53
  53.8 1.6 gather_fusion
  55.4 4.4 negate_convert_fusion
  59.8 0.3 fusion
  60.2 0.4 copy-done.4
  60.6 0.3 copy.13
  60.9 0.3 copy.16
  61.2 332.4 %all-reduce.3.cloned.1.call-done = (bf16[2,640,1024]{2,1,0:T(8,128)(2,1)}, bf16[2,640,1024]{2,1,0:T(8,128)(2,1)}, bf16[2,640,1024]{2,1,0:T(8,128)(2,1)}, bf16[2,640,1024]{2,1,0:T(8,128)(2,1)}) async-done(((bf16[2,640,1024]{2,1,0:T(8,128)(2,1)}, bf16[2,640,1024]{2,1,0:T(8,128)(2,1)}, bf16[2,640,1024]{2,1,0:T(8,128)(2,1)}, bf16[2,640,1024]{2,1,0:T(8,128)(2,1)}), (bf16[2,640,1024]{2,1,0:T(8,128)(2,1)}, ...) | async-done | bytes 10485776 | tf_op jit(solution)/shard_map/psum | solution.py:13
  393.7 3.5 multiply_convert_fusion.2
  397.2 1.5 multiply_convert_fusion.3
  398.8 0.2 copy-done.9
  398.9 1.5 multiply_convert_fusion.4
  400.5 0.2 copy-done.8
  400.7 1.5 multiply_convert_fusion.1
  402.2 0.8 pad_maximum_fusion
  403.0 0.6 fusion.17
  403.6 4.4 pad_maximum_fusion.1
  407.9 8.9 %copy.12 = bf16[16,640,256]{1,0,2:T(8,128)(2,1)} copy(bf16[16,640,256]{2,1,0:T(8,128)(2,1)} %get-tuple-element.34) | data formatting | bytes 10485760 | tf_op jit(solution)/shard_map/concatenate | solution.py:30
  416.9 4.9 fusion.19
  421.8 3.9 copy.14
  425.7 9.0 %copy.15 = bf16[16,640,256]{1,0,2:T(8,128)(2,1)} copy(bf16[16,640,256]{2,1,0:T(8,128)(2,1)} %get-tuple-element.35) | data formatting | bytes 10485760 | tf_op jit(solution)/shard_map/concatenate | solution.py:32
  434.7 4.9 fusion.20
  439.6 4.8 copy.17
  444.5 4.4 pad_maximum_fusion.3
  448.9 0.0 reduce-scatter.2.cloned.1.call-update
  448.9 74.8 %reduce-scatter.2.cloned.1.call-done = bf16[8,160,512]{2,1,0:T(8,128)(2,1)} async-done(((bf16[8,640,512]{2,1,0:T(8,128)(2,1)}), bf16[8,160,512]{2,1,0:T(8,128)(2,1)}) %reduce-scatter.2.cloned.1.call-update) | async-done | bytes 1310736 | tf_op jit(solution)/shard_map/reduce_scatter | solution.py:73
  523.7 4.4 multiply_convert_fusion
  (28 shorter events, 0.1 us)
Async XLA Ops:
  6.5 387.1 %all-reduce.3.cloned.1.call-start = ((), (), s32[]{:S(2)}) async-start(), calls=%async_computation.2 | async-start | bytes 20971520 | tf_op jit(solution)/shard_map/psum | solution.py:13
  45.4 2.7 copy-start
  48.1 2.7 copy-start.1
  52.7 0.7 copy-start.7
  52.7 471.0 %reduce-scatter.2.cloned.1.call-start = ((), (), s32[]{:S(2)}) async-start(), calls=%async_computation.1 | async-start | bytes 6553600 | tf_op jit(solution)/shard_map/reduce_scatter | solution.py:73
  59.8 0.8 copy-start.4
  59.8 340.7 %copy-start.2 = (bf16[1024,256]{1,0:T(8,128)(2,1)}, bf16[1024,256]{1,0:T(8,128)(2,1)S(1)}, u32[]{:S(2)}) copy-start(bf16[1024,256]{1,0:T(8,128)(2,1)S(1)} %get-tuple-element.51) | copy-start | bytes 1572868
  393.7 3.5 copy-start.5
  393.7 3.5 copy-start.10
  397.2 1.7 copy-start.9
  398.9 1.7 copy-start.8
  448.9 74.8 %copy-start.3 = (bf16[1024,256]{1,0:T(8,128)(2,1)S(1)}, bf16[1024,256]{1,0:T(8,128)(2,1)}, u32[]{:S(2)}) copy-start(bf16[1024,256]{1,0:T(8,128)(2,1)} %copy-done.2) | copy-start | bytes 1572868
  448.9 74.8 %copy-start.6 = (bf16[1024,256]{1,0:T(8,128)(2,1)S(1)}, bf16[1024,256]{1,0:T(8,128)(2,1)}, u32[]{:S(2)}) copy-start(bf16[1024,256]{1,0:T(8,128)(2,1)} %copy-done.4) | copy-start | bytes 1572868
Sparse Core Ops, SparseCore 0:
  52.8 340.8 all-reduce.2
  449.0 74.6 reduce-scatter.1
where the time goes:
time: 536 us; the launch traced here: 535 us
  waiting for transfers between devices  407 us (76%)
  local copies, waits for them, and re-layouts  56.9 us (11%)
  other arithmetic  23.9 us (4%)
  between operations  23.9 us (4%)
  matrix products  22.7 us (4%)
    psum x1, waiting for transfers between devices, spread(): return lax.psum(jnp.where(mine, array, jnp.zeros_like(array)), axis)  332 us
    reduce_scatter x1, waiting for transfers between devices, shards(): lax.psum_scatter(partial_value.astype(jnp.bfloat16), 'surf', scatter_dime...  74.8 us
    gather x4, local copies, waits for them, and re-layouts, shards(): picked = jnp.take(traces, wanted % shot_dev, axis=0)  23.2 us
  transfers between devices with their start and end apart: 2, of which 2 were waited for; matrix products, arithmetic and copies ran while one was open for 1% of the time, Pallas kernels for 0%

commit v1 on v0

v1 whole, which is shorter than its diff:
```python
import math

import jax
import jax.numpy as jnp
from jax import lax
from jax.sharding import PartitionSpec as P

F = 256


def dft_rows(samples, owners):
    bins = F // owners
    freq = jnp.arange(F, dtype=jnp.int32).reshape(owners, 1, bins, 1)
    time = jnp.arange(samples, dtype=jnp.int32)
    angles = (freq * time % samples).astype(jnp.float32) * (2.0 * math.pi / samples)
    table = jnp.concatenate([jnp.cos(angles), -jnp.sin(angles)], axis=1)
    return table.astype(jnp.bfloat16).reshape(2 * F, samples)


def shards(traces, surface_point, gather_index):
    shots, receivers, samples = traces.shape
    owners = lax.axis_size("shot")
    share = receivers // lax.axis_size("surf")
    bins = F // owners
    forward = dft_rows(samples, owners)
    factor = samples**-0.5
    points = surface_point.reshape(-1)
    sources = gather_index.reshape(-1)
    count = points.shape[0]
    block = lax.dynamic_slice_in_dim(traces, lax.axis_index("surf") * share, share, axis=1)
    rows = jnp.concatenate([block, jnp.take(traces, points, axis=1)], axis=1)
    spectra = lax.dot_general(
        forward, rows, (((1,), (2,)), ((), ())), preferred_element_type=jnp.float32
    )
    spectra = (spectra * factor).astype(jnp.bfloat16)
    spectra = spectra.reshape(owners, 2 * bins, shots, share + count)
    here = lax.all_to_all(spectra, "shot", 0, 0, tiled=True)
    here = here.reshape(owners, 2, bins, shots, share + count)
    far = here[sources // shots, :, :, sources % shots, :share]
    near = here[..., share:].transpose(2, 0, 3, 1, 4).reshape(bins, owners * shots, 2 * count)
    far = far.transpose(2, 1, 0, 3)
    right = jnp.concatenate(
        [
            jnp.concatenate([far[:, 0], far[:, 1]], axis=2),
            jnp.concatenate([-far[:, 1], far[:, 0]], axis=2),
        ],
        axis=1,
    )
    total = jnp.einsum("bsk,bkr->bsr", near, right, preferred_element_type=jnp.float32)
    total = total.astype(jnp.bfloat16).reshape(bins, owners, shots, 2, share)
    total = total.transpose(1, 3, 0, 2, 4).reshape(owners, 2 * bins, shots, share)
    back = lax.all_to_all(total, "shot", 0, 0, tiled=True)
    back = back.reshape(2 * F, shots, share)
    result = lax.dot_general(
        back, forward, (((0,), (0,)), ((), ())), preferred_element_type=jnp.float32
    )
    return (result * -factor).astype(jnp.bfloat16)


def solution(mesh):
    placed = (P("shot", None, None), P(), P())
    return jax.shard_map(
        shards, mesh=mesh, in_specs=placed, out_specs=P("shot", "surf", None), check_vma=False
    )
```

time: 536 us -> 163 us (0.30)
  waiting for transfers between devices: 407 us -> 26.1 us
  blocking collectives: 0 us -> 31.7 us
  local copies, waits for them, and re-layouts: 56.9 us -> 81.8 us
  between operations: 23.9 us -> 0.17 us
  other arithmetic: 23.9 us -> 5.14 us
  matrix products: 22.7 us -> 5.78 us
  starting transfers between devices: 0.22 us -> 9.54 us
    psum x1 -> x0, waiting for transfers between devices: 332 us -> none  [spread(): return lax.psum(jnp.where(mine, array, jnp.zeros_like(array)), axis)]
    reduce_scatter x1 -> x0, waiting for transfers between devices: 74.8 us -> none  [shards(): lax.psum_scatter(partial_value.astype(jnp.bfloat16), 'surf', scatter_dime...]
    reshape x2 -> x6, local copies, waits for them, and re-layouts: 0.17 us -> 44.3 us  [the longest x1 38.3 us: shards(): here = here.reshape(owners, 2, bins, shots, share + count)]
    all_to_all x0 -> x1, blocking collectives: none -> 31.7 us  [shards(): back = lax.all_to_all(total, 'shot', 0, 0, tiled=True)]
    all_to_all x0 -> x1, waiting for transfers between devices: none -> 26.1 us  [shards(): here = lax.all_to_all(spectra, 'shot', 0, 0, tiled=True)]
    concatenate x4 -> x0, local copies, waits for them, and re-layouts: 18.5 us -> none  [the longest x1 8.96 us: spectral_product(): right_imag = jnp.concatenate([far_imag, far_real], axis=0)]
    dot_general x8 -> x3, matrix products: 22.7 us -> 5.78 us  [the longest x1 3.11 us: shards(): lax.dot_general(back, forward, (((0,), (0,)), ((), ())), preferred_elemen...]
    select_n x7 -> x2, other arithmetic: 9.92 us -> 0.12 us  [shards(): rows = jnp.concatenate([block, jnp.take(traces, points, axis=1)], axis=1)]
  transfers between devices with their start and end apart: 2 -> 1, of which waited for: 2 -> 1; matrix products, arithmetic and copies ran while one was open for 1% -> 0% of each run, Pallas kernels for 0% -> 0%
where the time goes in v1:
time: 163 us; the launch traced here: 160 us
  local copies, waits for them, and re-layouts  81.8 us (50%)
  blocking collectives  31.7 us (19%)
  waiting for transfers between devices  26.1 us (16%)
  starting transfers between devices  9.54 us (6%)
  matrix products  5.78 us (4%)
  other arithmetic  5.14 us (3%)
    reshape x1, local copies, waits for them, and re-layouts, shards(): here = here.reshape(owners, 2, bins, shots, share + count)  38.3 us
    all_to_all x1, blocking collectives, shards(): back = lax.all_to_all(total, 'shot', 0, 0, tiled=True)  31.7 us
    all_to_all x1, waiting for transfers between devices, shards(): here = lax.all_to_all(spectra, 'shot', 0, 0, tiled=True)  26.1 us
    gather x2, local copies, waits for them, and re-layouts, shards(): far = here[sources // shots, :, :, sources % shots, :share]  24 us
    all_to_all x1, starting transfers between devices, shards(): here = lax.all_to_all(spectra, 'shot', 0, 0, tiled=True)  9.54 us
    reshape x1, local copies, waits for them, and re-layouts, shards(): total = total.astype(jnp.bfloat16).reshape(bins, owners, shots, 2, share)  5.25 us
    cos x1, other arithmetic, dft_rows(): table = jnp.concatenate([jnp.cos(angles), -jnp.sin(angles)], axis=1)  4.87 us
  transfers between devices with their start and end apart: 1, of which 1 were waited for; matrix products, arithmetic and copies ran while one was open for 0% of the time, Pallas kernels for 0%

profile of v1, /device:TPU:1, one launch (start us, length us, event | category | flops | bytes accessed | tf_op | source)
XLA Modules:
  0.0 160.2 jit_solution(7762981333815174041)
XLA Ops:
  0.0 0.8 copy.10
  0.8 0.1 reshape.287
  0.9 0.1 reshape.286
  1.0 4.9 %fusion.13 = (bf16[32,1,8,1024]{3,2,1,0:T(8,128)(2,1)S(1)}, bf16[32,1,8,1024]{3,2,1,0:T(8,128)(2,1)S(1)}) fusion(s32[32,8]{1,0:T(8,128)S(1)} %multiply_add_fusion), kind=kLoop, calls=%fused_computation.23 | loop fusion | flops 4456448 | bytes 1049600 | tf_op jit(solution)/shard_map/cos | solution.py:16
  5.9 2.5 %gather_fusion = bf16[32,8,1024]{2,0,1:T(8,128)(2,1)S(1)} fusion(bf16[8,640,1024]{2,1,0:T(8,128)(2,1)} %param.3, s32[1024]{0:T(1024)S(1)} %pad_clamp_fusion), kind=kCustom, calls=%fused_computation | custom fusion | bytes 1048704 | tf_op jit(solution)/shard_map/jit(_take)/gather | solution.py:31
  8.5 2.0 %constant_dynamic-slice_fusion = bf16[8,160,1024]{2,1,0:T(8,128)(2,1)S(1)} fusion(bf16[8,640,1024]{2,1,0:T(8,128)(2,1)} %param.3, s32[]{:T(128)S(6)} %select_n.89), kind=kLoop, calls=%fused_computation.52 | loop fusion | bytes 5242884 | tf_op jit(solution)/shard_map/dynamic_slice | solution.py:30
  10.5 0.1 select_bitcast_fusion
  10.6 0.1 maximum_convert_fusion
  10.7 0.0 copy-start
  10.7 1.0 copy-done
  11.7 1.8 %multiply_convert_fusion.1 = bf16[512,8,192]{0,2,1:T(8,128)(2,1)S(1)} fusion(bf16[512,1024,1]{1,0,2:T(8,128)(2,1)S(1)} %bitcast.34, bf16[8,32,1024]{2,1,0:T(8,128)(2,1)S(1)} %select_bitcast_fusion, bf16[8,160,1024]{2,1,0:T(8,128)(2,1)S(1)} %constant_dynamic-slice_fusion), kind=kOutput, calls=%fused_computation.7 | convolution fusion | flops 1618477056 | bytes 5767168 | tf_op jit(solution)/shard_map/dot_general | solution.py:32
  13.6 3.0 %copy.12 = bf16[512,8,192]{2,1,0:T(8,128)(2,1)} copy(bf16[512,8,192]{0,2,1:T(8,128)(2,1)S(1)} %multiply_convert_fusion.1) | data formatting | bytes 3145728 | tf_op jit(solution)/shard_map/convert_element_type | solution.py:35
  16.6 0.0 copy-start.2
  16.6 9.5 %all-to-all-start = ((bf16[32,16,8,192]{3,2,1,0:T(8,128)(2,1)}), bf16[32,16,8,192]{3,2,1,0:T(8,128)(2,1)S(1)}, u32[]{:S(2)}, u32[]{:S(2)}) async-start(bf16[32,16,8,192]{3,2,1,0:T(8,128)(2,1)} %bitcast.28), calls=%async_computation | async-start | bytes 4194304 | tf_op jit(solution)/shard_map/all_to_all | solution.py:37
  26.1 0.0 copy-done.2
  26.1 0.1 copy.14
  26.2 0.1 reshape.291
  26.4 26.1 %all-to-all-done = bf16[32,16,8,192]{3,2,1,0:T(8,128)(2,1)S(1)} async-done(((bf16[32,16,8,192]{3,2,1,0:T(8,128)(2,1)}), bf16[32,16,8,192]{3,2,1,0:T(8,128)(2,1)S(1)}, u32[]{:S(2)}, u32[]{:S(2)}) %all-to-all-start) | async-done | bytes 1572896 | tf_op jit(solution)/shard_map/all_to_all | solution.py:37
  52.5 0.4 slice_bitcast_fusion
  52.9 38.3 %copy.15 = bf16[32,2,8,8,192]{2,1,3,0,4:T(2,128)(2,1)} copy(bf16[32,2,8,8,192]{4,3,2,1,0:T(8,128)(2,1)S(1)} %bitcast.27) | data formatting | bytes 3145728 | tf_op jit(solution)/shard_map/reshape | solution.py:38
  91.2 18.2 %gather_fusion.1 = bf16[32,2,8,160]{2,1,3,0:T(2,128)(2,1)} fusion(bf16[32,2,8,8,192]{2,1,3,0,4:T(2,128)(2,1)} %copy.15, s32[32]{0:T(128)S(1)} %fusion.27), kind=kCustom, calls=%fused_computation.1 | custom fusion | bytes 328064 | tf_op jit(solution)/shard_map/gather | solution.py:39
  109.4 5.8 %copy.16 = bf16[32,2,8,160]{3,0,2,1:T(8,128)(2,1)S(1)} copy(bf16[32,2,8,160]{2,1,3,0:T(2,128)(2,1)} %gather_fusion.1) | data formatting | bytes 327680 | tf_op jit(solution)/shard_map/gather | solution.py:39
  115.3 1.6 %copy.13 = bf16[8,32,8,2,32]{4,3,2,1,0:T(2,128)(2,1)S(1)} copy(bf16[8,32,8,2,32]{4,2,0,3,1:T(8,128)(2,1)S(1)} %slice_bitcast_fusion) | data formatting | bytes 524288 | tf_op jit(solution)/shard_map/transpose | solution.py:40
  116.9 0.5 reshape.290
  117.4 0.8 convolution_convert_fusion
  118.2 1.6 copy.18
  119.8 5.2 %reshape.292 = bf16[8,32,8,2,160]{4,3,2,1,0:T(2,128)(2,1)S(1)} reshape(bf16[8,256,320]{2,1,0:T(8,128)(2,1)} %copy.18) | data formatting | bytes 2621440 | tf_op jit(solution)/shard_map/reshape | solution.py:50
  125.0 0.4 copy.19
  125.4 0.0 copy-start.1
  125.4 31.7 %all_to_all.10 = bf16[32,16,8,160]{3,2,1,0:T(8,128)(2,1)S(1)} all-to-all(bf16[32,16,8,160]{3,2,1,0:T(8,128)(2,1)S(1)} %bitcast.30), channel_id=1, replica_groups=mesh['surf'=4,'shot'=32] {'shot'}, dimensions={0} | all-to-all | bytes 2621440 | tf_op jit(solution)/shard_map/all_to_all | solution.py:52
  157.1 0.0 copy-done.1
  157.1 3.1 %multiply_convert_fusion = bf16[8,160,1024]{2,1,0:T(8,128)(2,1)} fusion(bf16[512,1024,1]{1,0,2:T(8,128)(2,1)S(1)} %bitcast.35, bf16[512,8,160]{2,1,0:T(8,128)(2,1)S(1)} %bitcast.31), kind=kOutput, calls=%fused_computation.2 | convolution fusion | flops 1344798720 | bytes 4980736 | tf_op jit(solution)/shard_map/dot_general | solution.py:54
  (7 shorter events, 0.1 us)
Async XLA Ops:
  10.7 1.1 copy-start
  16.6 9.5 %copy-start.2 = (s32[4,4,2]{1,2,0:T(2,128)S(1)}, s32[4,4,2]{1,2,0:T(2,128)}, u32[]{:S(2)}) copy-start(s32[4,4,2]{1,2,0:T(2,128)} %param.5) | copy-start | bytes 388
  16.6 35.9 %all-to-all-start = ((bf16[32,16,8,192]{3,2,1,0:T(8,128)(2,1)}), bf16[32,16,8,192]{3,2,1,0:T(8,128)(2,1)S(1)}, u32[]{:S(2)}, u32[]{:S(2)}) async-start(bf16[32,16,8,192]{3,2,1,0:T(8,128)(2,1)} %bitcast.28), calls=%async_computation | async-start | bytes 4194304 | tf_op jit(solution)/shard_map/all_to_all | solution.py:37
  125.4 31.7 %copy-start.1 = (bf16[32,2,8,1024]{3,2,1,0:T(8,128)(2,1)S(1)}, bf16[32,2,8,1024]{3,2,1,0:T(8,128)(2,1)}, u32[]{:S(2)}) copy-start(bf16[32,2,8,1024]{3,2,1,0:T(8,128)(2,1)} %copy-done) | copy-start | bytes 3145732

commit v2 on v1

v2 whole, which is shorter than its diff:
```python
import functools
import math

import jax
import jax.numpy as jnp
import ml_dtypes
import numpy as np
from jax import lax
from jax.experimental import pallas as pl
from jax.experimental.pallas import tpu as pltpu
from jax.sharding import PartitionSpec as P

F = 256
OWNERS = 32
BINS = F // OWNERS
PART = 2 * BINS
SHOTS = 8
POINTS = 32
MAIN, TAIL = 128, 32
SHARE = MAIN + TAIL
WIDE = SHOTS * TAIL
MESH = pl.DeviceIdType.MESH
F32, BF16 = jnp.float32, jnp.bfloat16


def dft_rows(samples):
    freq = np.arange(F).reshape(OWNERS, 1, BINS, 1)
    angles = (freq * np.arange(samples) % samples) * (2.0 * math.pi / samples)
    table = np.concatenate([np.cos(angles), -np.sin(angles)], axis=1)
    table = table.astype(np.float32).astype(ml_dtypes.bfloat16).astype(np.float32)
    scaled = table.reshape(2 * F, samples) * samples**-0.5
    return scaled.astype(ml_dtypes.bfloat16)


def offsets():
    steps = [(z, x, y) for z in range(2) for x in range(4) for y in range(4)][1:]
    return sorted(steps, key=lambda k: -(k[0] + min(k[1], 4 - k[1]) + min(k[2], 4 - k[2])))


def halves(array):
    return array[:, :MAIN], array[:, MAIN:]


def wide_rows(ref, rows):
    return jnp.concatenate([ref[half, rows, :] for half in range(2)], axis=1)


def dot(a, b, contract):
    return lax.dot_general(a, b, (contract, ((), ())), preferred_element_type=F32)


def kernel(
    points, gathers, traces, table, out,
    tab, xm, xt, full, xn, sm, sn, st, rm, rn, rt,
    near, far_main, far_tail, om, ot, bm, bt, hm, ht, ov,
    load_sem, own_sem, send_sem, recv_sem,
):
    group, me = lax.axis_index("surf"), lax.axis_index("shot")
    z, x, y = me // 16, (me // 4) % 4, me % 4
    peers = [(z ^ k) * 16 + (x + i) % 4 * 4 + (y + j) % 4 for k, i, j in offsets()]
    first = group * SHARE

    loads = [
        pltpu.make_async_copy(table, tab, load_sem.at[0]),
        pltpu.make_async_copy(traces.at[:, pl.ds(first, MAIN), :], xm, load_sem.at[1]),
        pltpu.make_async_copy(traces.at[:, pl.ds(first + MAIN, TAIL), :], xt, load_sem.at[2]),
        pltpu.make_async_copy(traces, full, load_sem.at[3]),
    ]
    for load in loads:
        load.start()
    barrier = pltpu.get_barrier_semaphore()
    for peer in peers:
        pl.semaphore_signal(barrier, inc=1, device_id=(group, peer), device_id_type=MESH)

    def exchange(kind, source, target):
        own = pltpu.make_async_copy(source.at[me], target(me), own_sem.at[kind])
        own.start()
        copies = [own]
        for k, peer in enumerate(peers):
            copy = pltpu.make_async_remote_copy(
                src_ref=source.at[peer],
                dst_ref=target(me),
                send_sem=send_sem.at[kind, k],
                recv_sem=recv_sem.at[kind, k],
                device_id=(group, peer),
                device_id_type=MESH,
            )
            copy.start()
            copies.append(copy)
        return copies

    def arrive(copies):
        copies[0].wait()
        for copy in copies[1:]:
            copy.wait_recv()

    def forward(rows):
        spectra = dot(tab[...], rows, ((1,), (1,))).astype(BF16)
        return spectra.reshape(OWNERS, PART, WIDE)

    loads[0].wait()
    loads[1].wait()
    for k in range(SHOTS // 2):
        spectra = forward(xm[2 * k : 2 * k + 2].reshape(WIDE, -1))
        for half, value in enumerate((spectra[..., :MAIN], spectra[..., MAIN:])):
            sm[:, 2 * k + half] = value
    pl.semaphore_wait(barrier, len(peers))
    mains = exchange(0, sm, lambda device: rm.at[pl.ds(device * SHOTS, SHOTS)])

    chosen = jnp.zeros((POINTS, 1), jnp.int32)
    position = lax.broadcasted_iota(jnp.int32, (POINTS, 1), 0)
    for i in range(POINTS):
        chosen = jnp.where(position == i, points[i], chosen)
    receivers = full.shape[1]
    pick = (lax.broadcasted_iota(jnp.int32, (POINTS, receivers), 1) == chosen).astype(BF16)
    loads[3].wait()
    for s in range(SHOTS):
        xn[s * POINTS : (s + 1) * POINTS, :] = dot(pick, full[s], ((1,), (0,))).astype(BF16)
    sn[...] = forward(xn[...])
    nears = exchange(1, sn, lambda device: rn.at[device])
    loads[2].wait()
    st[...] = forward(xt[...].reshape(WIDE, -1))
    tails = exchange(2, st, lambda device: rt.at[device])

    block = lambda axis: lax.broadcasted_iota(jnp.int32, (WIDE, WIDE), axis) // TAIL
    diagonal = (block(0) == block(1)).astype(BF16)
    tile = lambda a: jnp.concatenate([a] * SHOTS, axis=0)
    arrive(mains)
    for i in range(POINTS):
        far_main[i * PART : (i + 1) * PART, :] = rm[gathers[i]].astype(F32)
    arrive(nears)
    for half, value in enumerate(halves(rn[...].reshape(OWNERS * PART, WIDE))):
        near[half] = value.astype(F32)
    for b in range(BINS):
        rows = [pl.ds(b, OWNERS, stride=PART), pl.ds(BINS + b, OWNERS, stride=PART)]
        left = [tile(wide_rows(near, r).astype(BF16)) * diagonal for r in rows]
        real, imag = [tile(far_main[r, :].astype(BF16)) for r in rows]
        right = jnp.concatenate(
            [jnp.concatenate([real, imag], axis=1), jnp.concatenate([-imag, real], axis=1)], axis=0
        )
        total = -dot(jnp.concatenate(left, axis=1), right, ((1,), (0,)))
        for s in range(SHOTS):
            for part in range(2):
                om[pl.ds(s * PART + part * BINS + b, OWNERS, stride=SHOTS * PART), :] = total[
                    s * OWNERS : (s + 1) * OWNERS, part * MAIN : (part + 1) * MAIN
                ]
    totals = om[...].reshape(OWNERS, SHOTS, PART, MAIN)
    for s in range(SHOTS):
        bm[:, :, s * MAIN : (s + 1) * MAIN] = totals[:, s].astype(BF16)
    back_mains = exchange(3, bm, lambda device: hm.at[device])

    arrive(tails)
    fold = lambda axis: lax.broadcasted_iota(jnp.int32, (WIDE, WIDE), axis) % TAIL
    spread = (fold(0) == fold(1)).astype(BF16)
    shot_of = lax.broadcasted_iota(jnp.int32, (PART, WIDE), 1) // TAIL
    picked = []
    for i in range(POINTS):
        owner, local = lax.div(gathers[i], SHOTS), lax.rem(gathers[i], SHOTS)
        picked.append(rt[owner] * (shot_of == local).astype(BF16))
    for half, value in enumerate(halves(dot(jnp.concatenate(picked, axis=0), spread, ((1,), (0,))))):
        far_tail[half] = value
    for b in range(BINS):
        rows = [pl.ds(b, OWNERS, stride=PART), pl.ds(BINS + b, OWNERS, stride=PART)]
        left = jnp.concatenate([wide_rows(near, r).astype(BF16) for r in rows], axis=1)
        real, imag = [tile(wide_rows(far_tail, r).astype(BF16)) * diagonal for r in rows]
        right = jnp.concatenate(
            [jnp.concatenate([real, imag], axis=1), jnp.concatenate([-imag, real], axis=1)], axis=0
        )
        total = -dot(left, right, ((1,), (0,)))
        for part in range(2):
            for half in range(2):
                lanes = slice(part * WIDE + half * MAIN, part * WIDE + (half + 1) * MAIN)
                ot[half, rows[part], :] = total[:, lanes]
    for half in range(2):
        lanes = slice(half * MAIN, (half + 1) * MAIN)
        bt[:, :, lanes] = ot[half].reshape(OWNERS, PART, MAIN).astype(BF16)
    back_tails = exchange(4, bt, lambda device: ht.at[device])

    arrive(back_mains)
    for k in range(SHOTS // 2):
        spectrum = hm[:, :, k * WIDE : (k + 1) * WIDE].reshape(2 * F, WIDE)
        series = dot(spectrum, tab[...], ((0,), (0,))).astype(BF16)
        ov[2 * k : 2 * k + 2, :MAIN, :] = series.reshape(2, MAIN, -1)
    arrive(back_tails)
    series = dot(ht[...].reshape(2 * F, WIDE), tab[...], ((0,), (0,))).astype(BF16)
    ov[:, MAIN:, :] = series.reshape(SHOTS, TAIL, -1)
    store = pltpu.make_async_copy(ov, out, load_sem.at[0])
    store.start()
    for copies in (mains, nears, tails, back_mains, back_tails):
        for copy in copies[1:]:
            copy.wait_send()
    store.wait()


def shards(traces, surface_point, gather_index):
    shots, receivers, samples = traces.shape
    vmem = lambda *shape, dtype=BF16: pltpu.VMEM(shape, dtype)
    smem, hbm = pl.BlockSpec(memory_space=pltpu.SMEM), pl.BlockSpec(memory_space=pl.ANY)
    message = lambda lanes: vmem(OWNERS, PART, lanes)
    return pl.pallas_call(
        kernel,
        out_shape=jax.ShapeDtypeStruct((shots, SHARE, samples), BF16),
        in_specs=[smem, smem, hbm, hbm],
        out_specs=hbm,
        scratch_shapes=[
            vmem(2 * F, samples),
            vmem(SHOTS, MAIN, samples),
            vmem(SHOTS, TAIL, samples),
            vmem(SHOTS, receivers, samples),
            vmem(WIDE, samples),
            vmem(OWNERS, SHOTS, PART, MAIN),
            message(WIDE),
            message(WIDE),
            vmem(OWNERS * SHOTS, PART, MAIN),
            message(WIDE),
            message(WIDE),
            vmem(2, OWNERS * PART, MAIN, dtype=F32),
            vmem(POINTS * PART, MAIN, dtype=F32),
            vmem(2, POINTS * PART, MAIN, dtype=F32),
            vmem(OWNERS * SHOTS * PART, MAIN, dtype=F32),
            vmem(2, OWNERS * PART, MAIN, dtype=F32),
            *[message(lanes) for lanes in (SHOTS * MAIN, WIDE) * 2],
            vmem(SHOTS, SHARE, samples),
            pltpu.SemaphoreType.DMA((4,)),
            pltpu.SemaphoreType.DMA((5,)),
            pltpu.SemaphoreType.DMA((5, OWNERS - 1)),
            pltpu.SemaphoreType.DMA((5, OWNERS - 1)),
        ],
        compiler_params=pltpu.CompilerParams(
            collective_id=0, has_side_effects=True, vmem_limit_bytes=56 * 2**20
        ),
    )(surface_point.reshape(-1), gather_index.reshape(-1), traces, jnp.asarray(dft_rows(samples)))


def solution(mesh):
    placed = (P("shot", None, None), P(), P())
    return jax.shard_map(
        shards, mesh=mesh, in_specs=placed, out_specs=P("shot", "surf", None), check_vma=False
    )
```

time: 163 us -> 54.7 us (0.34); the launches traced: 160 us -> 54.5 us
  local copies, waits for them, and re-layouts: 81.8 us -> 6.27 us
  Pallas kernels: 0 us -> 48.2 us
  blocking collectives: 31.7 us -> 0 us
  waiting for transfers between devices: 26.1 us -> 0 us
  starting transfers between devices: 9.54 us -> 0 us
  matrix products: 5.78 us -> 0 us
  other arithmetic: 5.14 us -> 0 us
    pallas_call x0 -> x1, Pallas kernels: none -> 48.2 us  [shards(): pl.pallas_call(kernel, out_shape=jax.ShapeDtypeStruct((shots, SHARE, samp...]
    reshape x6 -> x2, local copies, waits for them, and re-layouts: 44.3 us -> 1.22 us  [the longest x1 0.62 us: shards(): gather_index.reshape(-1)]
    all_to_all x1 -> x0, blocking collectives: 31.7 us -> none  [shards(): back = lax.all_to_all(total, 'shot', 0, 0, tiled=True)]
    gather x3 -> x0, local copies, waits for them, and re-layouts: 26.6 us -> none  [the longest x2 24 us: shards(): far = here[sources // shots, :, :, sources % shots, :share]]
    all_to_all x1 -> x0, waiting for transfers between devices: 26.1 us -> none  [shards(): here = lax.all_to_all(spectra, 'shot', 0, 0, tiled=True)]
    all_to_all x1 -> x0, starting transfers between devices: 9.54 us -> none  [shards(): here = lax.all_to_all(spectra, 'shot', 0, 0, tiled=True)]
    dot_general x3 -> x0, matrix products: 5.78 us -> none  [the longest x1 3.11 us: shards(): lax.dot_general(back, forward, (((0,), (0,)), ((), ())), preferred_elemen...]
    cos x1 -> x0, other arithmetic: 4.87 us -> none  [dft_rows(): table = jnp.concatenate([jnp.cos(angles), -jnp.sin(angles)], axis=1)]
  transfers between devices with their start and end apart: 1 -> 0, of which waited for: 1 -> 0; matrix products, arithmetic and copies ran while one was open for 0% -> 0% of each run, Pallas kernels for 0% -> 0%
where the time goes in v2:
time: 54.7 us; the launch traced here: 54.5 us
  Pallas kernels  48.2 us (88%)
  local copies, waits for them, and re-layouts  6.27 us (11%)
    pallas_call x1, Pallas kernels, shards(): pl.pallas_call(kernel, out_shape=jax.ShapeDtypeStruct((shots, SHARE, samp...  48.2 us
    unnamed x3, local copies, waits for them, and re-layouts  5.05 us

profile of v2, /device:TPU:1, one launch (start us, length us, event | category | flops | bytes accessed | tf_op | source)
XLA Modules:
  0.0 54.5 jit_solution(5670832083413474188)
XLA Ops:
  0.0 0.8 %copy.7 = s32[4,4,2]{2,1,0:T(4,128)S(1)} copy(s32[4,4,2]{1,2,0:T(2,128)} %param.5) | data formatting | bytes 256 | tf_op args[1]
  0.8 0.6 %reshape.6.points = s32[32]{0:T(128)} reshape(s32[4,4,2]{2,1,0:T(4,128)S(1)} %copy.7) | data formatting | bytes 256 | tf_op jit(solution)/shard_map/reshape | solution.py:232
  1.4 0.8 %copy.8 = s32[4,4,2]{2,1,0:T(4,128)S(1)} copy(s32[4,4,2]{1,2,0:T(2,128)} %param.6) | data formatting | bytes 256 | tf_op args[2]
  2.2 0.6 %reshape.7.gathers = s32[32]{0:T(128)} reshape(s32[4,4,2]{2,1,0:T(4,128)S(1)} %copy.8) | data formatting | bytes 256 | tf_op jit(solution)/shard_map/reshape | solution.py:232
  2.8 48.2 %shard_map.46 = bf16[8,160,1024]{2,1,0:T(8,128)(2,1)} custom-call(s32[32]{0:T(128)} %reshape.6.points, s32[32]{0:T(128)} %reshape.7.gathers, bf16[8,640,1024]{2,1,0:T(8,128)(2,1)} %traces.1, bf16[512,1024]{1,0:T(8,128)(2,1)} %constant.2.clone.table), custom_call_target="tpu_custom_call" | custom-call | tf_op jit(solution)/shard_map/pallas_call | solution.py:200
  51.1 3.5 %copy.10 = bf16[8,160,1024]{2,1,0:T(8,128)(2,1)} copy(bf16[8,160,1024]{2,1,0:T(8,128)(2,1)} %shard_map.46) | data formatting | bytes 5242880

commit v3 on v1

v3 whole, which is shorter than its diff:
```python
import functools
import math

import jax
import jax.numpy as jnp
import ml_dtypes
import numpy as np
from jax import lax
from jax.experimental import pallas as pl
from jax.experimental.pallas import tpu as pltpu
from jax.sharding import PartitionSpec as P

F = 256
OWNERS = 32
BINS = F // OWNERS
PART = 2 * BINS
SHOTS = 8
POINTS = 32
MAIN, TAIL = 128, 32
SHARE = MAIN + TAIL
HALF = POINTS // 2
WIDE = SHOTS * TAIL
MESH = pl.DeviceIdType.MESH
F32, BF16 = jnp.float32, jnp.bfloat16


def dft_rows(samples):
    freq = np.arange(F).reshape(OWNERS, 1, BINS, 1)
    angles = (freq * np.arange(samples) % samples) * (2.0 * math.pi / samples)
    table = np.concatenate([np.cos(angles), -np.sin(angles)], axis=1)
    table = table.astype(np.float32).astype(ml_dtypes.bfloat16).astype(np.float32)
    scaled = table.reshape(2 * F, samples) * samples**-0.5
    return scaled.astype(ml_dtypes.bfloat16)


def offsets():
    steps = [(z, x, y) for z in range(2) for x in range(4) for y in range(4)][1:]
    return sorted(steps, key=lambda k: -(k[0] + min(k[1], 4 - k[1]) + min(k[2], 4 - k[2])))


def wide_rows(ref, rows):
    return jnp.concatenate([ref[half, rows, :] for half in range(2)], axis=1)


def dot(a, b, contract):
    return lax.dot_general(a, b, (contract, ((), ())), preferred_element_type=F32)


def iota(shape, axis):
    return lax.broadcasted_iota(jnp.int32, shape, axis)


def product(left, right):
    real, imag = right
    both = jnp.concatenate(
        [jnp.concatenate([real, imag], axis=1), jnp.concatenate([-imag, real], axis=1)], axis=0
    )
    return dot(left, both, ((1,), (0,)))


def kernel(
    point_ref, gather_ref, traces, table, hm, ht,
    points, gathers, tab, full, xn, sm, sn, st, rm, rn, other, rt,
    near, lhs, far_main, far_tail, om, ot, bm, bt,
    load_sem, pair_sem, ready, send_sem, recv_sem,
):
    group, me = lax.axis_index("surf"), lax.axis_index("shot")
    core = group % 2
    z, x, y = me // 16, (me // 4) % 4, me % 4
    peers = [(z ^ k) * 16 + (x + i) % 4 * 4 + (y + j) % 4 for k, i, j in offsets()]
    away = lambda d: [n for n, step in enumerate(offsets()) if sum(map(bool, step)) == d]
    groups = lax.axis_size("surf")

    share = SHARE // PART
    blocks = [pl.ds((group + k) % groups * share, share) for k in range(groups)]
    loads = [pltpu.make_async_copy(table, tab, load_sem.at[0])]
    for k, block in enumerate(blocks):
        loads.append(pltpu.make_async_copy(traces.at[:, block], full.at[:, block], load_sem.at[1 + k]))
    loads.append(pltpu.make_async_copy(point_ref, points, load_sem.at[5]))
    loads.append(pltpu.make_async_copy(gather_ref, gathers, load_sem.at[6]))
    for load in loads:
        load.start()
    barrier = pltpu.get_barrier_semaphore()
    greetings = [barrier, ready.at[0], ready.at[1]]

    def greet(stage):
        for n in away(1):
            pl.semaphore_signal(
                greetings[stage], inc=1, device_id=(group, peers[n]), device_id_type=MESH
            )

    pl.semaphore_signal(barrier, inc=1, device_id=(group ^ 1, me), device_id_type=MESH)
    greet(0)

    def start(way, which):
        kind, source, target = way
        for n in which:
            pltpu.make_async_remote_copy(
                src_ref=source(peers[n]),
                dst_ref=target(me),
                send_sem=send_sem.at[kind],
                recv_sem=recv_sem.at[kind],
                device_id=(group, peers[n]),
                device_id_type=MESH,
            ).start()

    def keep(way):
        kind, source, target = way
        pltpu.make_async_copy(source(me), target(me), recv_sem.at[kind]).start()

    def arrive(kind, whole):
        pltpu.make_async_copy(whole, whole, recv_sem.at[kind]).wait()

    def sent(kind, whole):
        others = whole.at[pl.ds(0, OWNERS - 1)]
        pltpu.make_async_copy(others, others, send_sem.at[kind]).wait()

    def forward(rows):
        spectra = dot(tab[...], rows, ((1,), (1,))).astype(BF16)
        return spectra.reshape(OWNERS, PART, -1)

    slot = lambda ref: lambda device: ref.at[device]
    two = lambda ref, k: lambda device: ref.at[device, pl.ds(2 * k, 2)]
    pairs = range(SHOTS // 2)
    everyone = away(3) + away(2) + away(1)
    tail_way, near_way = (0, slot(st), slot(rt)), (1, slot(sn), slot(rn))
    main_ways = [(2, two(sm, k), two(rm, k)) for k in pairs]

    loads[0].wait()
    loads[1].wait()
    own = group * share
    main = pl.ds(own, MAIN // PART)
    tail = pl.ds(own + MAIN // PART, TAIL // PART)
    st[...] = forward(full[:, tail].reshape(WIDE, -1))
    for k in pairs:
        spectra = forward(full[2 * k : 2 * k + 2, main].reshape(2 * MAIN, -1))
        sm[:, 2 * k] = spectra[..., :MAIN]
        sm[:, 2 * k + 1] = spectra[..., MAIN:]
    for way in (tail_way, *main_ways):
        keep(way)
    pl.semaphore_wait(barrier, len(away(1)) + 1)
    greet(1)
    for way in (tail_way, *main_ways):
        start(way, away(1))

    for load in loads[2:]:
        load.wait()
    chosen = jnp.zeros((HALF, 1), jnp.int32)
    aligned = []
    for i in range(HALF):
        point = points[core * 2 + i // 8, i // 4 % 2, i % 4]
        aligned.append(lax.div(point, PART))
        chosen = jnp.where(iota((HALF, 1), 0) == i, i * PART + lax.rem(point, PART), chosen)
    pick = (iota((HALF, HALF * PART), 1) == chosen).astype(BF16)
    for s in range(SHOTS):
        rows = jnp.concatenate([full[s, row] for row in aligned], axis=0)
        xn[s * HALF : (s + 1) * HALF, :] = dot(pick, rows, ((1,), (0,))).astype(BF16)
    sn[...] = forward(xn[...])
    keep(near_way)
    start(near_way, away(1))
    pl.semaphore_wait(greetings[1], len(away(1)))
    greet(2)
    for way in (tail_way, near_way, *main_ways[:2]):
        start(way, away(2))
    pl.semaphore_wait(greetings[2], len(away(1)))
    for way in (tail_way, near_way):
        start(way, away(3))
    for way in main_ways[:2]:
        start(way, away(3))
    for way in main_ways[2:]:
        start(way, away(3) + away(2))

    lines = [[pl.ds(part * BINS + b, OWNERS, stride=PART) for part in range(2)] for b in range(BINS)]
    local_of = iota((PART, WIDE), 1) // TAIL
    spread = (iota((WIDE, WIDE), 0) % TAIL == iota((WIDE, WIDE), 1) % TAIL).astype(BF16)
    shot_of_point = lambda axis: iota((WIDE, WIDE), axis) % MAIN // HALF
    tile = lambda a: jnp.concatenate([a[:HALF]] * SHOTS + [a[HALF:]] * SHOTS, axis=0)
    index = lambda i: gathers[i // 8, i // 4 % 2, i % 4]

    arrive(0, rt)
    picked = []
    for i in range(POINTS):
        mask = (local_of == lax.rem(index(i), SHOTS)).astype(BF16)
        picked.append(rt[lax.div(index(i), SHOTS)] * mask)
    spectra = dot(jnp.concatenate(picked, axis=0), spread, ((1,), (0,)))
    for half in range(2):
        far_tail[half] = spectra[:, half * MAIN : (half + 1) * MAIN]
    arrive(1, rn)
    swap = pltpu.make_async_remote_copy(
        src_ref=rn,
        dst_ref=other,
        send_sem=pair_sem.at[0],
        recv_sem=pair_sem.at[1],
        device_id=(group ^ 1, me),
        device_id_type=MESH,
    )
    swap.start()
    near[core] = rn[...].reshape(OWNERS * PART, MAIN).astype(F32)
    swap.wait()
    near[1 - core] = other[...].reshape(OWNERS * PART, MAIN).astype(F32)
    diagonal = (shot_of_point(0) == iota((WIDE, WIDE), 1) // TAIL).astype(BF16)
    for b in range(BINS):
        left = jnp.concatenate([wide_rows(near, r).astype(BF16) for r in lines[b]], axis=1)
        right = [tile(wide_rows(far_tail, r).astype(BF16)) * diagonal for r in lines[b]]
        total = -product(left, right)
        for part in range(2):
            for half in range(2):
                lanes = slice(part * WIDE + half * MAIN, part * WIDE + (half + 1) * MAIN)
                ot[half, lines[b][part], :] = total[:, lanes]
    for half in range(2):
        lanes = slice(half * MAIN, (half + 1) * MAIN)
        bt[:, :, lanes] = ot[half].reshape(OWNERS, PART, MAIN).astype(BF16)
    back_tail = 3, slot(bt), slot(ht)
    keep(back_tail)
    start(back_tail, everyone)
    diagonal = (iota((WIDE, WIDE), 0) // OWNERS == shot_of_point(1)).astype(BF16)
    for b in range(BINS):
        for part, r in enumerate(lines[b]):
            copies = [wide_rows(near, r).astype(BF16)] * SHOTS
            lhs[b, :, part * WIDE : (part + 1) * WIDE] = jnp.concatenate(copies, axis=0) * diagonal

    arrive(2, rm)
    for i in range(POINTS):
        far = rm[lax.div(index(i), SHOTS), lax.rem(index(i), SHOTS)]
        far_main[i * PART : (i + 1) * PART, :] = far.astype(F32)
    for b in range(BINS):
        total = -product(lhs[b], [tile(far_main[r, :].astype(BF16)) for r in lines[b]])
        for s in range(SHOTS):
            for part in range(2):
                om[pl.ds(s * PART + part * BINS + b, OWNERS, stride=SHOTS * PART), :] = total[
                    s * OWNERS : (s + 1) * OWNERS, part * MAIN : (part + 1) * MAIN
                ]
    totals = om[...].reshape(OWNERS, SHOTS, PART, MAIN)
    for k in pairs:
        bm[:, 2 * k : 2 * k + 2] = totals[:, 2 * k : 2 * k + 2].astype(BF16)
        back_main = 4, two(bm, k), two(hm, k)
        keep(back_main)
        start(back_main, everyone)
    arrive(3, ht)
    arrive(4, hm)
    for kind, whole in enumerate((st, sn, sm, bt, bm)):
        sent(kind, whole)


def inverse(hm, ht, table, out, hm_v, ht_v, tab, series, load_sem, store_sem):
    shots = out.shape[0]
    pairs = range(shots // 2)
    loads = [
        pltpu.make_async_copy(table, tab, load_sem.at[0]),
        pltpu.make_async_copy(ht, ht_v, load_sem.at[1]),
        *[
            pltpu.make_async_copy(hm.at[:, pl.ds(2 * k, 2)], hm_v.at[k], load_sem.at[2 + k])
            for k in pairs
        ],
    ]
    for load in loads:
        load.start()
    invert = lambda spectra: dot(spectra, tab[...], ((0,), (0,))).astype(BF16)
    loads[0].wait()
    loads[1].wait()
    series[:, MAIN:, :] = invert(ht_v[...].reshape(2 * F, WIDE)).reshape(shots, TAIL, -1)
    stores = []
    for k in pairs:
        loads[2 + k].wait()
        two = pl.ds(2 * k, 2)
        spectra = [hm_v[k, :, s].reshape(2 * F, MAIN) for s in range(2)]
        series[two, :MAIN, :] = invert(jnp.concatenate(spectra, axis=1)).reshape(2, MAIN, -1)
        stores.append(pltpu.make_async_copy(series.at[two], out.at[two], store_sem.at[k]))
        stores[-1].start()
    for store in stores:
        store.wait()


def shards(traces, surface_point, gather_index):
    shots, receivers, samples = traces.shape
    vmem = lambda *shape, dtype=BF16: pltpu.VMEM(shape, dtype)
    hbm, anywhere = pl.BlockSpec(memory_space=pltpu.HBM), pl.BlockSpec(memory_space=pl.ANY)
    message = lambda lanes: vmem(OWNERS, PART, lanes)
    table = jnp.asarray(dft_rows(samples))
    back = [
        jax.ShapeDtypeStruct((OWNERS, SHOTS, PART, MAIN), BF16),
        jax.ShapeDtypeStruct((OWNERS, PART, WIDE), BF16),
    ]
    spectra = pl.pallas_call(
        kernel,
        out_shape=back,
        in_specs=[hbm] * 4,
        out_specs=[anywhere, anywhere],
        scratch_shapes=[
            pltpu.SMEM((4, 2, 4), jnp.int32),
            pltpu.SMEM((4, 2, 4), jnp.int32),
            vmem(2 * F, samples),
            vmem(SHOTS, receivers // PART, PART, samples),
            vmem(SHOTS * HALF, samples),
            vmem(OWNERS, SHOTS, PART, MAIN),
            message(MAIN),
            message(WIDE),
            vmem(OWNERS, SHOTS, PART, MAIN),
            message(MAIN),
            message(MAIN),
            message(WIDE),
            vmem(2, OWNERS * PART, MAIN, dtype=F32),
            vmem(BINS, WIDE, 2 * WIDE),
            vmem(POINTS * PART, MAIN, dtype=F32),
            vmem(2, POINTS * PART, MAIN, dtype=F32),
            vmem(OWNERS * SHOTS * PART, MAIN, dtype=F32),
            vmem(2, OWNERS * PART, MAIN, dtype=F32),
            vmem(OWNERS, SHOTS, PART, MAIN),
            message(WIDE),
            pltpu.SemaphoreType.DMA((7,)),
            pltpu.SemaphoreType.DMA((2,)),
            pltpu.SemaphoreType.REGULAR((2,)),
            pltpu.SemaphoreType.DMA((5,)),
            pltpu.SemaphoreType.DMA((5,)),
        ],
        compiler_params=pltpu.CompilerParams(
            collective_id=0, has_side_effects=True, vmem_limit_bytes=61 * 2**20
        ),
    )(
        surface_point.transpose(0, 2, 1),
        gather_index.transpose(0, 2, 1),
        traces.reshape(shots, receivers // PART, PART, samples),
        table,
    )
    return pl.pallas_call(
        inverse,
        out_shape=jax.ShapeDtypeStruct((shots, SHARE, samples), BF16),
        in_specs=[anywhere] * 3,
        out_specs=anywhere,
        scratch_shapes=[
            vmem(SHOTS // 2, OWNERS, 2, PART, MAIN),
            message(WIDE),
            vmem(2 * F, samples),
            vmem(SHOTS, SHARE, samples),
            pltpu.SemaphoreType.DMA((2 + SHOTS // 2,)),
            pltpu.SemaphoreType.DMA((SHOTS // 2,)),
        ],
        compiler_params=pltpu.CompilerParams(vmem_limit_bytes=61 * 2**20),
    )(*spectra, table)


def solution(mesh):
    placed = (P("shot", None, None), P(), P())
    return jax.shard_map(
        shards, mesh=mesh, in_specs=placed, out_specs=P("shot", "surf", None), check_vma=False
    )
```

time: 163 us -> 48.2 us (0.30); the launches traced: 160 us -> 47.5 us
  local copies, waits for them, and re-layouts: 81.8 us -> 0 us
  Pallas kernels: 0 us -> 47.5 us
  blocking collectives: 31.7 us -> 0 us
  waiting for transfers between devices: 26.1 us -> 0 us
  starting transfers between devices: 9.54 us -> 0 us
  matrix products: 5.78 us -> 0 us
  other arithmetic: 5.14 us -> 0 us
    pallas_call x0 -> x2, Pallas kernels: none -> 47.5 us  [the longest x1 43 us: shards(): pl.pallas_call(kernel, out_shape=back, in_specs=[hbm] * 4, out_specs=[any...]
    reshape x6 -> x0, local copies, waits for them, and re-layouts: 44.3 us -> none  [the longest x1 38.3 us: shards(): here = here.reshape(owners, 2, bins, shots, share + count)]
    all_to_all x1 -> x0, blocking collectives: 31.7 us -> none  [shards(): back = lax.all_to_all(total, 'shot', 0, 0, tiled=True)]
    gather x3 -> x0, local copies, waits for them, and re-layouts: 26.6 us -> none  [the longest x2 24 us: shards(): far = here[sources // shots, :, :, sources % shots, :share]]
    all_to_all x1 -> x0, waiting for transfers between devices: 26.1 us -> none  [shards(): here = lax.all_to_all(spectra, 'shot', 0, 0, tiled=True)]
    all_to_all x1 -> x0, starting transfers between devices: 9.54 us -> none  [shards(): here = lax.all_to_all(spectra, 'shot', 0, 0, tiled=True)]
    dot_general x3 -> x0, matrix products: 5.78 us -> none  [the longest x1 3.11 us: shards(): lax.dot_general(back, forward, (((0,), (0,)), ((), ())), preferred_elemen...]
    cos x1 -> x0, other arithmetic: 4.87 us -> none  [dft_rows(): table = jnp.concatenate([jnp.cos(angles), -jnp.sin(angles)], axis=1)]
  transfers between devices with their start and end apart: 1 -> 0, of which waited for: 1 -> 0; matrix products, arithmetic and copies ran while one was open for 0% -> 0% of each run, Pallas kernels for 0% -> 0%
where the time goes in v3:
time: 48.2 us; the launch traced here: 47.5 us
  Pallas kernels  47.5 us (99%)
    pallas_call x1, Pallas kernels, shards(): pl.pallas_call(kernel, out_shape=back, in_specs=[hbm] * 4, out_specs=[any...  43 us
    pallas_call x1, Pallas kernels, shards(): pl.pallas_call(inverse, out_shape=jax.ShapeDtypeStruct((shots, SHARE, sam...  4.5 us

profile of v3, /device:TPU:1, one launch (start us, length us, event | category | flops | bytes accessed | tf_op | source)
XLA Modules:
  0.0 47.5 jit_solution(16792001358923917946)
XLA Ops:
  0.0 43.0 %shard_map.46 = (bf16[32,8,16,128]{3,2,1,0:T(8,128)(2,1)}, bf16[32,16,256]{2,1,0:T(8,128)(2,1)}) custom-call(s32[4,2,4]{2,1,0:T(2,128)} %bitcast.4, s32[4,2,4]{2,1,0:T(2,128)} %bitcast.5, bf16[8,40,16,1024]{3,2,1,0:T(8,128)(2,1)} %bitcast.3, bf16[512,1024]{1,0:T(8,128)(2,1)} %constant.2.clone.table), custom_call_target="tpu_custom_call" | custom-call | tf_op jit(solution)/shard_map/pallas_call | solution.py:284
  43.0 4.5 %shard_map.47 = bf16[8,160,1024]{2,1,0:T(8,128)(2,1)} custom-call(bf16[32,8,16,128]{3,2,1,0:T(8,128)(2,1)} %get-tuple-element.7.hm, bf16[32,16,256]{2,1,0:T(8,128)(2,1)} %get-tuple-element.8.ht, bf16[512,1024]{1,0:T(8,128)(2,1)} %constant.2.clone.table), custom_call_target="tpu_custom_call" | custom-call | tf_op jit(solution)/shard_map/pallas_call | solution.py:325

commit v4 on v3

--- a/solution.py
+++ b/solution.py
@@ -84,7 +84,7 @@
     greetings = [barrier, ready.at[0], ready.at[1]]
 
     def greet(stage):
-        for n in away(1):
+        for n in away(1) + away(2) + away(3) if stage == 0 else []:
             pl.semaphore_signal(
                 greetings[stage], inc=1, device_id=(group, peers[n]), device_id_type=MESH
             )
@@ -138,10 +138,10 @@
         sm[:, 2 * k + 1] = spectra[..., MAIN:]
     for way in (tail_way, *main_ways):
         keep(way)
-    pl.semaphore_wait(barrier, len(away(1)) + 1)
+    pl.semaphore_wait(barrier, 32)
     greet(1)
-    for way in (tail_way, *main_ways):
-        start(way, away(1))
+    for way in (tail_way, *main_ways[:2]):
+        start(way, everyone)
 
     for load in loads[2:]:
         load.wait()
@@ -157,18 +157,9 @@
         xn[s * HALF : (s + 1) * HALF, :] = dot(pick, rows, ((1,), (0,))).astype(BF16)
     sn[...] = forward(xn[...])
     keep(near_way)
-    start(near_way, away(1))
-    pl.semaphore_wait(greetings[1], len(away(1)))
-    greet(2)
-    for way in (tail_way, near_way, *main_ways[:2]):
-        start(way, away(2))
-    pl.semaphore_wait(greetings[2], len(away(1)))
-    for way in (tail_way, near_way):
-        start(way, away(3))
-    for way in main_ways[:2]:
-        start(way, away(3))
+    start(near_way, everyone)
     for way in main_ways[2:]:
-        start(way, away(3) + away(2))
+        start(way, everyone)
 
     lines = [[pl.ds(part * BINS + b, OWNERS, stride=PART) for part in range(2)] for b in range(BINS)]
     local_of = iota((PART, WIDE), 1) // TAIL

time: 48.2 us -> 46 us (0.954)
  Pallas kernels: 47.5 us -> 45.2 us
    pallas_call x1, Pallas kernels: 43 us -> 40.8 us  [shards(): pl.pallas_call(kernel, out_shape=back, in_specs=[hbm] * 4, out_specs=[any...]
where the time goes in v4:
time: 46 us; the launch traced here: 45.3 us
  Pallas kernels  45.2 us (98%)
    pallas_call x1, Pallas kernels, shards(): pl.pallas_call(kernel, out_shape=back, in_specs=[hbm] * 4, out_specs=[any...  40.8 us
    pallas_call x1, Pallas kernels, shards(): pl.pallas_call(inverse, out_shape=jax.ShapeDtypeStruct((shots, SHARE, sam...  4.5 us

profile of v4, /device:TPU:1, one launch (start us, length us, event | category | flops | bytes accessed | tf_op | source)
XLA Modules:
  0.0 45.3 jit_solution(16513358726519705340)
XLA Ops:
  0.0 40.8 %shard_map.46 = (bf16[32,8,16,128]{3,2,1,0:T(8,128)(2,1)}, bf16[32,16,256]{2,1,0:T(8,128)(2,1)}) custom-call(s32[4,2,4]{2,1,0:T(2,128)} %bitcast.4, s32[4,2,4]{2,1,0:T(2,128)} %bitcast.5, bf16[8,40,16,1024]{3,2,1,0:T(8,128)(2,1)} %bitcast.3, bf16[512,1024]{1,0:T(8,128)(2,1)} %constant.2.clone.table), custom_call_target="tpu_custom_call" | custom-call | tf_op jit(solution)/shard_map/pallas_call | solution.py:275
  40.8 4.5 %shard_map.47 = bf16[8,160,1024]{2,1,0:T(8,128)(2,1)} custom-call(bf16[32,8,16,128]{3,2,1,0:T(8,128)(2,1)} %get-tuple-element.7.hm, bf16[32,16,256]{2,1,0:T(8,128)(2,1)} %get-tuple-element.8.ht, bf16[512,1024]{1,0:T(8,128)(2,1)} %constant.2.clone.table), custom_call_target="tpu_custom_call" | custom-call | tf_op jit(solution)/shard_map/pallas_call | solution.py:316

commit v5 on v4

--- a/solution.py
+++ b/solution.py
@@ -21,11 +21,12 @@
 HALF = POINTS // 2
 WIDE = SHOTS * TAIL
 MESH = pl.DeviceIdType.MESH
+ROOMS = (4, 6, 8)
 F32, BF16 = jnp.float32, jnp.bfloat16
 
 
 def dft_rows(samples):
-    freq = np.arange(F).reshape(OWNERS, 1, BINS, 1)
+    freq = np.arange(F).reshape(OWNERS // 2, BINS, 2).transpose(2, 0, 1).reshape(OWNERS, 1, BINS, 1)
     angles = (freq * np.arange(samples) % samples) * (2.0 * math.pi / samples)
     table = np.concatenate([np.cos(angles), -np.sin(angles)], axis=1)
     table = table.astype(np.float32).astype(ml_dtypes.bfloat16).astype(np.float32)
@@ -59,42 +60,42 @@
 
 
 def kernel(
+    slots,
     point_ref, gather_ref, traces, table, hm, ht,
-    points, gathers, tab, full, xn, sm, sn, st, rm, rn, other, rt,
+    points, gathers, slot_v, slot_of, tab, block, full, xn, sm, sn, st, rm, rn, other, rt,
     near, lhs, far_main, far_tail, om, ot, bm, bt,
-    load_sem, pair_sem, ready, send_sem, recv_sem,
+    load_sem, pair_sem, send_sem, recv_sem,
 ):
     group, me = lax.axis_index("surf"), lax.axis_index("shot")
     core = group % 2
     z, x, y = me // 16, (me // 4) % 4, me % 4
     peers = [(z ^ k) * 16 + (x + i) % 4 * 4 + (y + j) % 4 for k, i, j in offsets()]
     away = lambda d: [n for n, step in enumerate(offsets()) if sum(map(bool, step)) == d]
+    everyone = away(3) + away(2) + away(1)
     groups = lax.axis_size("surf")
 
     share = SHARE // PART
     blocks = [pl.ds((group + k) % groups * share, share) for k in range(groups)]
-    loads = [pltpu.make_async_copy(table, tab, load_sem.at[0])]
-    for k, block in enumerate(blocks):
-        loads.append(pltpu.make_async_copy(traces.at[:, block], full.at[:, block], load_sem.at[1 + k]))
+    loads = [
+        pltpu.make_async_copy(table, tab, load_sem.at[0]),
+        pltpu.make_async_copy(traces.at[:, blocks[0]], block, load_sem.at[1]),
+    ]
+    for k in range(1, groups):
+        part = traces.at[:, blocks[k]], full.at[:, blocks[k]]
+        loads.append(pltpu.make_async_copy(*part, load_sem.at[1 + k]))
     loads.append(pltpu.make_async_copy(point_ref, points, load_sem.at[5]))
     loads.append(pltpu.make_async_copy(gather_ref, gathers, load_sem.at[6]))
     for load in loads:
         load.start()
     barrier = pltpu.get_barrier_semaphore()
-    greetings = [barrier, ready.at[0], ready.at[1]]
-
-    def greet(stage):
-        for n in away(1) + away(2) + away(3) if stage == 0 else []:
-            pl.semaphore_signal(
-                greetings[stage], inc=1, device_id=(group, peers[n]), device_id_type=MESH
-            )
-
     pl.semaphore_signal(barrier, inc=1, device_id=(group ^ 1, me), device_id_type=MESH)
-    greet(0)
-
-    def start(way, which):
+    for n in everyone:
+        pl.semaphore_signal(barrier, inc=1, device_id=(group, peers[n]), device_id_type=MESH)
+
+    def start(way):
         kind, source, target = way
-        for n in which:
+        pltpu.make_async_copy(source(me), target(me), recv_sem.at[kind]).start()
+        for n in everyone:
             pltpu.make_async_remote_copy(
                 src_ref=source(peers[n]),
                 dst_ref=target(me),
@@ -104,10 +105,6 @@
                 device_id_type=MESH,
             ).start()
 
-    def keep(way):
-        kind, source, target = way
-        pltpu.make_async_copy(source(me), target(me), recv_sem.at[kind]).start()
-
     def arrive(kind, whole):
         pltpu.make_async_copy(whole, whole, recv_sem.at[kind]).wait()
 
@@ -121,29 +118,57 @@
 
     slot = lambda ref: lambda device: ref.at[device]
     two = lambda ref, k: lambda device: ref.at[device, pl.ds(2 * k, 2)]
+    rounds = range(slots // 2)
+    early = 0 if slots == ROOMS[0] else 1
     pairs = range(SHOTS // 2)
-    everyone = away(3) + away(2) + away(1)
     tail_way, near_way = (0, slot(st), slot(rt)), (1, slot(sn), slot(rn))
-    main_ways = [(2, two(sm, k), two(rm, k)) for k in pairs]
+    main_ways = [(2, two(sm, k), two(rm, k)) for k in rounds]
+
+    for load in loads[5:]:
+        load.wait()
+    index = lambda i: gathers[i // 8, i // 4 % 2, i % 4]
+    owner = lambda i: lax.div(index(i), SHOTS)
+    if slots < SHOTS:
+        device = iota((SHOTS, MAIN), 1) * SHOTS + iota((SHOTS, MAIN), 0)
+        wanted = jnp.zeros((SHOTS, MAIN), jnp.int32)
+        for i in range(POINTS):
+            wanted = jnp.where(device == index(i), 1, wanted)
+        before = jnp.zeros((1, MAIN), jnp.int32)
+        for l in range(SHOTS):
+            row = wanted[l : l + 1]
+            slot_v[l : l + 1] = before + SHOTS * row
+            before = before + row
+        table_copy = pltpu.make_async_copy(slot_v, slot_of, load_sem.at[7])
+        table_copy.start()
+        table_copy.wait()
+        mine = [0] * SHOTS
+        for l in range(SHOTS):
+            for k in range(slots):
+                mine[k] = jnp.where(slot_of[l, me] == SHOTS + k, l, mine[k])
+        place = lambda i: slot_of[lax.rem(index(i), SHOTS), owner(i)] - SHOTS
+    else:
+        mine = range(SHOTS)
+        place = lambda i: lax.rem(index(i), SHOTS)
 
     loads[0].wait()
     loads[1].wait()
-    own = group * share
-    main = pl.ds(own, MAIN // PART)
-    tail = pl.ds(own + MAIN // PART, TAIL // PART)
-    st[...] = forward(full[:, tail].reshape(WIDE, -1))
-    for k in pairs:
-        spectra = forward(full[2 * k : 2 * k + 2, main].reshape(2 * MAIN, -1))
+    spread_own = pltpu.make_async_copy(block, full.at[:, blocks[0]], load_sem.at[8])
+    spread_own.start()
+    main, tail = pl.ds(0, MAIN // PART), pl.ds(MAIN // PART, TAIL // PART)
+    tails = st.shape[2] // TAIL
+    rows = [block[mine[k], tail].reshape(TAIL, -1) for k in range(tails)]
+    st[...] = forward(jnp.concatenate(rows, axis=0))
+    for k in rounds:
+        rows = [block[mine[2 * k + j], main].reshape(MAIN, -1) for j in range(2)]
+        spectra = forward(jnp.concatenate(rows, axis=0))
         sm[:, 2 * k] = spectra[..., :MAIN]
         sm[:, 2 * k + 1] = spectra[..., MAIN:]
-    for way in (tail_way, *main_ways):
-        keep(way)
-    pl.semaphore_wait(barrier, 32)
-    greet(1)
-    for way in (tail_way, *main_ways[:2]):
-        start(way, everyone)
-
-    for load in loads[2:]:
+
+    pl.semaphore_wait(barrier, len(everyone) + 1)
+    for way in (tail_way, *main_ways[:early]):
+        start(way)
+
+    for load in (*loads[2:5], spread_own):
         load.wait()
     chosen = jnp.zeros((HALF, 1), jnp.int32)
     aligned = []
@@ -156,23 +181,20 @@
         rows = jnp.concatenate([full[s, row] for row in aligned], axis=0)
         xn[s * HALF : (s + 1) * HALF, :] = dot(pick, rows, ((1,), (0,))).astype(BF16)
     sn[...] = forward(xn[...])
-    keep(near_way)
-    start(near_way, everyone)
-    for way in main_ways[2:]:
-        start(way, everyone)
+    for way in (near_way, *main_ways[early:]):
+        start(way)
 
     lines = [[pl.ds(part * BINS + b, OWNERS, stride=PART) for part in range(2)] for b in range(BINS)]
-    local_of = iota((PART, WIDE), 1) // TAIL
-    spread = (iota((WIDE, WIDE), 0) % TAIL == iota((WIDE, WIDE), 1) % TAIL).astype(BF16)
+    slot_at = iota((PART, st.shape[2]), 1) // TAIL
+    wide = (st.shape[2], WIDE)
+    spread = (iota(wide, 0) % TAIL == iota(wide, 1) % TAIL).astype(BF16)
     shot_of_point = lambda axis: iota((WIDE, WIDE), axis) % MAIN // HALF
     tile = lambda a: jnp.concatenate([a[:HALF]] * SHOTS + [a[HALF:]] * SHOTS, axis=0)
-    index = lambda i: gathers[i // 8, i // 4 % 2, i % 4]
 
     arrive(0, rt)
     picked = []
     for i in range(POINTS):
-        mask = (local_of == lax.rem(index(i), SHOTS)).astype(BF16)
-        picked.append(rt[lax.div(index(i), SHOTS)] * mask)
+        picked.append(rt[owner(i)] * (slot_at == place(i)).astype(BF16))
     spectra = dot(jnp.concatenate(picked, axis=0), spread, ((1,), (0,)))
     for half in range(2):
         far_tail[half] = spectra[:, half * MAIN : (half + 1) * MAIN]
@@ -202,8 +224,7 @@
         lanes = slice(half * MAIN, (half + 1) * MAIN)
         bt[:, :, lanes] = ot[half].reshape(OWNERS, PART, MAIN).astype(BF16)
     back_tail = 3, slot(bt), slot(ht)
-    keep(back_tail)
-    start(back_tail, everyone)
+    start(back_tail)
     diagonal = (iota((WIDE, WIDE), 0) // OWNERS == shot_of_point(1)).astype(BF16)
     for b in range(BINS):
         for part, r in enumerate(lines[b]):
@@ -212,8 +233,7 @@
 
     arrive(2, rm)
     for i in range(POINTS):
-        far = rm[lax.div(index(i), SHOTS), lax.rem(index(i), SHOTS)]
-        far_main[i * PART : (i + 1) * PART, :] = far.astype(F32)
+        far_main[i * PART : (i + 1) * PART, :] = rm[owner(i), place(i)].astype(F32)
     for b in range(BINS):
         total = -product(lhs[b], [tile(far_main[r, :].astype(BF16)) for r in lines[b]])
         for s in range(SHOTS):
@@ -225,8 +245,7 @@
     for k in pairs:
         bm[:, 2 * k : 2 * k + 2] = totals[:, 2 * k : 2 * k + 2].astype(BF16)
         back_main = 4, two(bm, k), two(hm, k)
-        keep(back_main)
-        start(back_main, everyone)
+        start(back_main)
     arrive(3, ht)
     arrive(4, hm)
     for kind, whole in enumerate((st, sn, sm, bt, bm)):
@@ -234,7 +253,7 @@
 
 
 def inverse(hm, ht, table, out, hm_v, ht_v, tab, series, load_sem, store_sem):
-    shots = out.shape[0]
+    shots, _, samples = out.shape
     pairs = range(shots // 2)
     loads = [
         pltpu.make_async_copy(table, tab, load_sem.at[0]),
@@ -246,20 +265,31 @@
     ]
     for load in loads:
         load.start()
-    invert = lambda spectra: dot(spectra, tab[...], ((0,), (0,))).astype(BF16)
+
+    def invert(spectra, two, receivers):
+        even = dot(spectra[:F], tab[:F], ((0,), (0,)))
+        odd = dot(spectra[F:], tab[F:], ((0,), (0,)))
+        shape = (two.stop - two.start, receivers.stop - receivers.start, samples // 2)
+        series[two, receivers, : samples // 2] = (even + odd).astype(BF16).reshape(shape)
+        series[two, receivers, samples // 2 :] = (even - odd).astype(BF16).reshape(shape)
+
     loads[0].wait()
     loads[1].wait()
-    series[:, MAIN:, :] = invert(ht_v[...].reshape(2 * F, WIDE)).reshape(shots, TAIL, -1)
+    invert(ht_v[...].reshape(2 * F, WIDE), slice(0, shots), slice(MAIN, SHARE))
     stores = []
     for k in pairs:
         loads[2 + k].wait()
         two = pl.ds(2 * k, 2)
         spectra = [hm_v[k, :, s].reshape(2 * F, MAIN) for s in range(2)]
-        series[two, :MAIN, :] = invert(jnp.concatenate(spectra, axis=1)).reshape(2, MAIN, -1)
+        invert(jnp.concatenate(spectra, axis=1), slice(2 * k, 2 * k + 2), slice(0, MAIN))
         stores.append(pltpu.make_async_copy(series.at[two], out.at[two], store_sem.at[k]))
         stores[-1].start()
     for store in stores:
         store.wait()
+
+
+def tail_lanes(slots):
+    return MAIN if slots * TAIL <= MAIN else WIDE
 
 
 def shards(traces, surface_point, gather_index):
@@ -267,29 +297,32 @@
     vmem = lambda *shape, dtype=BF16: pltpu.VMEM(shape, dtype)
     hbm, anywhere = pl.BlockSpec(memory_space=pltpu.HBM), pl.BlockSpec(memory_space=pl.ANY)
     message = lambda lanes: vmem(OWNERS, PART, lanes)
-    table = jnp.asarray(dft_rows(samples))
+    table = dft_rows(samples)
     back = [
         jax.ShapeDtypeStruct((OWNERS, SHOTS, PART, MAIN), BF16),
         jax.ShapeDtypeStruct((OWNERS, PART, WIDE), BF16),
     ]
-    spectra = pl.pallas_call(
-        kernel,
+    product = lambda slots: pl.pallas_call(
+        functools.partial(kernel, slots),
         out_shape=back,
         in_specs=[hbm] * 4,
         out_specs=[anywhere, anywhere],
         scratch_shapes=[
             pltpu.SMEM((4, 2, 4), jnp.int32),
             pltpu.SMEM((4, 2, 4), jnp.int32),
+            vmem(SHOTS, MAIN, dtype=jnp.int32),
+            pltpu.SMEM((SHOTS, MAIN), jnp.int32),
             vmem(2 * F, samples),
+            vmem(SHOTS, SHARE // PART, PART, samples),
             vmem(SHOTS, receivers // PART, PART, samples),
             vmem(SHOTS * HALF, samples),
-            vmem(OWNERS, SHOTS, PART, MAIN),
+            vmem(OWNERS, slots, PART, MAIN),
             message(MAIN),
-            message(WIDE),
-            vmem(OWNERS, SHOTS, PART, MAIN),
+            message(tail_lanes(slots)),
+            vmem(OWNERS, slots, PART, MAIN),
             message(MAIN),
             message(MAIN),
-            message(WIDE),
+            message(tail_lanes(slots)),
             vmem(2, OWNERS * PART, MAIN, dtype=F32),
             vmem(BINS, WIDE, 2 * WIDE),
             vmem(POINTS * PART, MAIN, dtype=F32),
@@ -298,21 +331,22 @@
             vmem(2, OWNERS * PART, MAIN, dtype=F32),
             vmem(OWNERS, SHOTS, PART, MAIN),
             message(WIDE),
-            pltpu.SemaphoreType.DMA((7,)),
+            pltpu.SemaphoreType.DMA((9,)),
             pltpu.SemaphoreType.DMA((2,)),
-            pltpu.SemaphoreType.REGULAR((2,)),
             pltpu.SemaphoreType.DMA((5,)),
             pltpu.SemaphoreType.DMA((5,)),
         ],
         compiler_params=pltpu.CompilerParams(
-            collective_id=0, has_side_effects=True, vmem_limit_bytes=61 * 2**20
+            collective_id=slots // 2, has_side_effects=True, vmem_limit_bytes=61 * 2**20
         ),
-    )(
-        surface_point.transpose(0, 2, 1),
-        gather_index.transpose(0, 2, 1),
-        traces.reshape(shots, receivers // PART, PART, samples),
-        table,
     )
+    points, gathers = surface_point.transpose(0, 2, 1), gather_index.transpose(0, 2, 1)
+    blocks = traces.reshape(shots, receivers // PART, PART, samples)
+    numbers = jnp.arange(OWNERS * SHOTS, dtype=jnp.int32).reshape(OWNERS, SHOTS)
+    wanted = jnp.any(gathers[..., None, None] == numbers, axis=(0, 1, 2))
+    most = jnp.max(jnp.sum(wanted.astype(jnp.int32), axis=1))
+    case = sum((most > room).astype(jnp.int32) for room in ROOMS[:-1])
+    spectra = lax.switch(case, [product(room) for room in ROOMS], points, gathers, blocks, jnp.asarray(table))
     return pl.pallas_call(
         inverse,
         out_shape=jax.ShapeDtypeStruct((shots, SHARE, samples), BF16),
@@ -321,13 +355,13 @@
         scratch_shapes=[
             vmem(SHOTS // 2, OWNERS, 2, PART, MAIN),
             message(WIDE),
-            vmem(2 * F, samples),
+            vmem(2 * F, samples // 2),
             vmem(SHOTS, SHARE, samples),
             pltpu.SemaphoreType.DMA((2 + SHOTS // 2,)),
             pltpu.SemaphoreType.DMA((SHOTS // 2,)),
         ],
         compiler_params=pltpu.CompilerParams(vmem_limit_bytes=61 * 2**20),
-    )(*spectra, table)
+    )(*spectra, jnp.asarray(table[:, : samples // 2]))
 
 
 def solution(mesh):

time: 46 us -> 43.1 us (0.937); the launches traced: 45.3 us -> 42.9 us
  Pallas kernels: 45.2 us -> 39.7 us
  between operations: 0.01 us -> 1.52 us
  other arithmetic: 0 us -> 1.45 us
    pallas_call x1, Pallas kernels: 40.8 us -> 36.1 us  [shards(): lax.switch(case, [product(room) for room in ROOMS], points, gathers, bloc...]
    pallas_call x1, Pallas kernels: 4.5 us -> 3.6 us  [shards(): pl.pallas_call(inverse, out_shape=jax.ShapeDtypeStruct((shots, SHARE, sam...]
    reduce_or x0 -> x1, other arithmetic: none -> 0.79 us  [shards(): wanted = jnp.any(gathers[..., None, None] == numbers, axis=(0, 1, 2))]
    reduce_max x0 -> x1, other arithmetic: none -> 0.64 us  [shards(): most = jnp.max(jnp.sum(wanted.astype(jnp.int32), axis=1))]
where the time goes in v5:
time: 43.1 us; the launch traced here: 42.9 us
  Pallas kernels  39.7 us (92%)
  between operations  1.52 us (4%)
  other arithmetic  1.45 us (3%)
    pallas_call x1, Pallas kernels, shards(): lax.switch(case, [product(room) for room in ROOMS], points, gathers, bloc...  36.1 us
    pallas_call x1, Pallas kernels, shards(): pl.pallas_call(inverse, out_shape=jax.ShapeDtypeStruct((shots, SHARE, sam...  3.6 us

profile of v5, /device:TPU:1, one launch (start us, length us, event | category | flops | bytes accessed | tf_op | source)
XLA Modules:
  0.0 42.9 jit_solution(12889878835940020623)
XLA Ops:
  0.0 0.8 %compare_reduce_fusion = pred[32,8]{0,1:T(8,128)(4,1)S(1)} fusion(s32[32,8]{0,1:T(8,128)S(1)} %multiply_add_fusion, s32[4,2,4]{2,1,0:T(2,128)} %bitcast.6), kind=kLoop, calls=%fused_computation | loop fusion | flops 16128 | bytes 1408 | tf_op jit(solution)/shard_map/reduce_or | solution.py:346
  0.8 0.6 %reduce_max.9 = s32[]{:T(128)} reduce(s32[32]{0:T(128)S(1)} %convert_reduce_fusion, s32[]{:T(128)} %constant.6.clone.1), dimensions={0}, to_apply=%region_2.0 | reduce | flops 31 | bytes 136 | tf_op jit(solution)/shard_map/reduce_max | solution.py:347
  2.8 36.3 %conditional.1 = ((bf16[32,8,16,128]{3,2,1,0:T(8,128)(2,1)S(1)}, bf16[32,16,256]{2,1,0:T(8,128)(2,1)S(1)})) conditional(s32[]{:T(128)} %clamp.3, (s32[4,2,4]{2,1,0:T(2,128)}, s32[4,2,4]{2,1,0:T(2,128)}, bf16[8,40,16,1024]{3,2,1,0:T(8,128)(2,1)}, bf16[512,1024]{1,0:T(8,128)(2,1)}) %tuple.27, (s32[4,2,4]{2,1,0:T(2,128)}, ...), branch_computations={%region_3.0_spmd, %region_4.0_spmd, %region_5.0_spmd} | conditional | bytes 8 | solution.py:349
  2.8 36.1 %branch_0_fun.1 = (bf16[32,8,16,128]{3,2,1,0:T(8,128)(2,1)S(1)}, bf16[32,16,256]{2,1,0:T(8,128)(2,1)S(1)}) custom-call(s32[4,2,4]{2,1,0:T(2,128)} %get-tuple-element.29.point_ref, s32[4,2,4]{2,1,0:T(2,128)} %get-tuple-element.30.gather_ref, bf16[8,40,16,1024]{3,2,1,0:T(8,128)(2,1)} %get-tuple-element.31.traces, bf16[512,1024]{1,0:T(8,128)(2,1)} %get-tuple-element.32.table), custom_call_target="tpu_custom_call" | custom-call | tf_op jit(solution)/shard_map/cond/branch_0_fun/pallas_call | solution.py:349
  39.1 3.6 %shard_map.55 = bf16[8,160,1024]{2,1,0:T(8,128)(2,1)} custom-call(bf16[32,8,16,128]{3,2,1,0:T(8,128)(2,1)S(1)} %get-tuple-element.43.hm, bf16[32,16,256]{2,1,0:T(8,128)(2,1)S(1)} %get-tuple-element.44.ht, bf16[512,512]{1,0:T(8,128)(2,1)} %constant.19.clone.table), custom_call_target="tpu_custom_call" | custom-call | tf_op jit(solution)/shard_map/pallas_call | solution.py:350
  (2 shorter events, 0.0 us)

commit v6 on v5

--- a/solution.py
+++ b/solution.py
@@ -129,10 +129,7 @@
     index = lambda i: gathers[i // 8, i // 4 % 2, i % 4]
     owner = lambda i: lax.div(index(i), SHOTS)
     if slots < SHOTS:
-        device = iota((SHOTS, MAIN), 1) * SHOTS + iota((SHOTS, MAIN), 0)
-        wanted = jnp.zeros((SHOTS, MAIN), jnp.int32)
-        for i in range(POINTS):
-            wanted = jnp.where(device == index(i), 1, wanted)
+        wanted = wanted_of(index)
         before = jnp.zeros((1, MAIN), jnp.int32)
         for l in range(SHOTS):
             row = wanted[l : l + 1]
@@ -252,20 +249,23 @@
         sent(kind, whole)
 
 
-def inverse(hm, ht, table, out, hm_v, ht_v, tab, series, load_sem, store_sem):
+def wanted_of(index):
+    gather = iota((SHOTS, MAIN), 1) * SHOTS + iota((SHOTS, MAIN), 0)
+    wanted = jnp.zeros((SHOTS, MAIN), jnp.int32)
+    for i in range(POINTS):
+        wanted = jnp.where(gather == index(i), 1, wanted)
+    return wanted
+
+
+def choose(gathers, case):
+    wanted = wanted_of(lambda i: gathers[i // 8, i // 4 % 2, i % 4])
+    most = jnp.max(jnp.sum(wanted, axis=0, keepdims=True))
+    case[0] = sum((most > room).astype(jnp.int32) for room in ROOMS[:-1])
+
+
+def inverse(hm, ht, tab, out, series, store_sem):
     shots, _, samples = out.shape
     pairs = range(shots // 2)
-    loads = [
-        pltpu.make_async_copy(table, tab, load_sem.at[0]),
-        pltpu.make_async_copy(ht, ht_v, load_sem.at[1]),
-        *[
-            pltpu.make_async_copy(hm.at[:, pl.ds(2 * k, 2)], hm_v.at[k], load_sem.at[2 + k])
-            for k in pairs
-        ],
-    ]
-    for load in loads:
-        load.start()
-
     def invert(spectra, two, receivers):
         even = dot(spectra[:F], tab[:F], ((0,), (0,)))
         odd = dot(spectra[F:], tab[F:], ((0,), (0,)))
@@ -273,14 +273,11 @@
         series[two, receivers, : samples // 2] = (even + odd).astype(BF16).reshape(shape)
         series[two, receivers, samples // 2 :] = (even - odd).astype(BF16).reshape(shape)
 
-    loads[0].wait()
-    loads[1].wait()
-    invert(ht_v[...].reshape(2 * F, WIDE), slice(0, shots), slice(MAIN, SHARE))
+    invert(ht[...].reshape(2 * F, WIDE), slice(0, shots), slice(MAIN, SHARE))
     stores = []
     for k in pairs:
-        loads[2 + k].wait()
         two = pl.ds(2 * k, 2)
-        spectra = [hm_v[k, :, s].reshape(2 * F, MAIN) for s in range(2)]
+        spectra = [hm[:, 2 * k + s].reshape(2 * F, MAIN) for s in range(2)]
         invert(jnp.concatenate(spectra, axis=1), slice(2 * k, 2 * k + 2), slice(0, MAIN))
         stores.append(pltpu.make_async_copy(series.at[two], out.at[two], store_sem.at[k]))
         stores[-1].start()
@@ -337,30 +334,28 @@
             pltpu.SemaphoreType.DMA((5,)),
         ],
         compiler_params=pltpu.CompilerParams(
-            collective_id=slots // 2, has_side_effects=True, vmem_limit_bytes=61 * 2**20
+            collective_id=slots // 2, has_side_effects=True, vmem_limit_bytes=50 * 2**20
         ),
     )
     points, gathers = surface_point.transpose(0, 2, 1), gather_index.transpose(0, 2, 1)
     blocks = traces.reshape(shots, receivers // PART, PART, samples)
-    numbers = jnp.arange(OWNERS * SHOTS, dtype=jnp.int32).reshape(OWNERS, SHOTS)
-    wanted = jnp.any(gathers[..., None, None] == numbers, axis=(0, 1, 2))
-    most = jnp.max(jnp.sum(wanted.astype(jnp.int32), axis=1))
-    case = sum((most > room).astype(jnp.int32) for room in ROOMS[:-1])
+    case = pl.pallas_call(
+        choose,
+        out_shape=jax.ShapeDtypeStruct((1,), jnp.int32),
+        in_specs=[pl.BlockSpec(memory_space=pltpu.SMEM)],
+        out_specs=pl.BlockSpec(memory_space=pltpu.SMEM),
+    )(gathers)[0]
     spectra = lax.switch(case, [product(room) for room in ROOMS], points, gathers, blocks, jnp.asarray(table))
     return pl.pallas_call(
         inverse,
         out_shape=jax.ShapeDtypeStruct((shots, SHARE, samples), BF16),
-        in_specs=[anywhere] * 3,
+        in_specs=[pl.BlockSpec(memory_space=pltpu.VMEM)] * 3,
         out_specs=anywhere,
         scratch_shapes=[
-            vmem(SHOTS // 2, OWNERS, 2, PART, MAIN),
-            message(WIDE),
-            vmem(2 * F, samples // 2),
             vmem(SHOTS, SHARE, samples),
-            pltpu.SemaphoreType.DMA((2 + SHOTS // 2,)),
             pltpu.SemaphoreType.DMA((SHOTS // 2,)),
         ],
-        compiler_params=pltpu.CompilerParams(vmem_limit_bytes=61 * 2**20),
+        compiler_params=pltpu.CompilerParams(vmem_limit_bytes=50 * 2**20),
     )(*spectra, jnp.asarray(table[:, : samples // 2]))
 
 

time: 43.1 us -> 41.2 us (0.956)
  other arithmetic: 1.45 us -> 0 us
  between operations: 1.52 us -> 0.88 us
    pallas_call x1, Pallas kernels: 3.6 us -> 1.99 us  [shards(): pl.pallas_call(inverse, out_shape=jax.ShapeDtypeStruct((shots, SHARE, sam...]
    pallas_call x0 -> x1, Pallas kernels: none -> 1.46 us  [shards(): pl.pallas_call(choose, out_shape=jax.ShapeDtypeStruct((1,), jnp.int32), i...]
    reduce_or x1 -> x0, other arithmetic: 0.79 us -> none  [shards(): wanted = jnp.any(gathers[..., None, None] == numbers, axis=(0, 1, 2))]
    reduce_max x1 -> x0, other arithmetic: 0.64 us -> none  [shards(): most = jnp.max(jnp.sum(wanted.astype(jnp.int32), axis=1))]
where the time goes in v6:
time: 41.2 us; the launch traced here: 41.1 us
  Pallas kernels  39.9 us (97%)
  between operations  0.88 us (2%)
    pallas_call x1, Pallas kernels, shards(): lax.switch(case, [product(room) for room in ROOMS], points, gathers, bloc...  36.5 us
    pallas_call x1, Pallas kernels, shards(): pl.pallas_call(inverse, out_shape=jax.ShapeDtypeStruct((shots, SHARE, sam...  1.99 us
    pallas_call x1, Pallas kernels, shards(): pl.pallas_call(choose, out_shape=jax.ShapeDtypeStruct((1,), jnp.int32), i...  1.46 us

profile of v6, /device:TPU:1, one launch (start us, length us, event | category | flops | bytes accessed | tf_op | source)
XLA Modules:
  0.0 41.1 jit_solution(3651598875192143181)
XLA Ops:
  0.0 1.5 %shard_map.55 = s32[1]{0:T(128)} custom-call(s32[4,2,4]{2,1,0:T(2,128)} %bitcast.7), custom_call_target="tpu_custom_call" | custom-call | tf_op jit(solution)/shard_map/pallas_call | solution.py:342
  2.1 0.0 copy-start
  2.1 36.8 %conditional.1 = ((bf16[32,8,16,128]{3,2,1,0:T(8,128)(2,1)S(1)}, bf16[32,16,256]{2,1,0:T(8,128)(2,1)S(1)})) conditional(s32[]{:T(128)} %bitcast.1, (s32[4,2,4]{2,1,0:T(2,128)}, s32[4,2,4]{2,1,0:T(2,128)}, bf16[8,40,16,1024]{3,2,1,0:T(8,128)(2,1)}, bf16[512,1024]{1,0:T(8,128)(2,1)}) %tuple.27, (s32[4,2,4]{2,1,0:T(2,128)}, ...), branch_computations={%region_0.0_spmd, %region_1.0_spmd, %region_2.0_spmd} | conditional | bytes 8 | solution.py:348
  2.1 36.5 %branch_0_fun.1 = (bf16[32,8,16,128]{3,2,1,0:T(8,128)(2,1)S(1)}, bf16[32,16,256]{2,1,0:T(8,128)(2,1)S(1)}) custom-call(s32[4,2,4]{2,1,0:T(2,128)} %get-tuple-element.29.point_ref, s32[4,2,4]{2,1,0:T(2,128)} %get-tuple-element.30.gather_ref, bf16[8,40,16,1024]{3,2,1,0:T(8,128)(2,1)} %get-tuple-element.31.traces, bf16[512,1024]{1,0:T(8,128)(2,1)} %get-tuple-element.32.table), custom_call_target="tpu_custom_call" | custom-call | tf_op jit(solution)/shard_map/cond/branch_0_fun/pallas_call | solution.py:348
  38.9 0.0 copy-done
  38.9 2.0 %shard_map.56 = bf16[8,160,1024]{2,1,0:T(8,128)(2,1)} custom-call(bf16[32,8,16,128]{3,2,1,0:T(8,128)(2,1)S(1)} %get-tuple-element.43.hm, bf16[32,16,256]{2,1,0:T(8,128)(2,1)S(1)} %get-tuple-element.44.ht, bf16[512,512]{1,0:T(8,128)(2,1)S(1)} %copy-done), custom_call_target="tpu_custom_call" | custom-call | tf_op jit(solution)/shard_map/pallas_call | solution.py:349
Async XLA Ops:
  2.1 36.8 %copy-start = (bf16[512,512]{1,0:T(8,128)(2,1)S(1)}, bf16[512,512]{1,0:T(8,128)(2,1)}, u32[]{:S(2)}) copy-start(bf16[512,512]{1,0:T(8,128)(2,1)} %constant.11.clone.tab) | copy-start | bytes 1572868
